TPU v7x, 32 devices: a whole 2x2x4 slice. The times are simulated.
32 devices in a mesh: feat: 8 (over z, x), tgt: 4 (over y, core).
Axes of the slice: x: 2, y: 2, z: 4, core: 2. Of those that a mesh axis runs over, the one named last changes fastest.
Arguments:
- sources: bfloat16 [4, 128, 2304], P('tgt'), may hold values from -6 to 6
- targets: bfloat16 [4, 128, 2304], P('tgt', 'feat'), may hold values from -6 to 6
- enc_weight: bfloat16 [4, 2304, 16384], P('tgt', None, 'feat'), may hold values from -0.125 to 0.125
- enc_bias: float32 [4, 16384], P('tgt', 'feat'), may hold values from -5 to 5
- dec_weight: bfloat16 [4, 4, 16384, 2304], P('tgt', None, 'feat'), may hold values from -0.046875 to 0.046875
- pair_mask: int32 [4, 4], replicated, may hold values from 0 to 1, as said below
Outputs:
- error: bfloat16 [4, 128, 2304], P('tgt', 'feat')
- latent_grad: bfloat16 [4, 128, 16384], P('tgt', None, 'feat')
Inputs may be any that keep to these rules, and one draw needn't show every extreme that they name: pair_mask[t, s] is 0 wherever s > t and 1 wherever s == t.
All inputs are finite; a program needn't handle non-finite values.
Results may differ from a plain program's by a relative error of at most 0.0055.
Values may be sent and summed in bfloat16 or wider, within the bound.
A program may use at most 128 MiB of HBM per device.

v0:
```python
import jax
import jax.numpy as jnp
from jax import lax
from jax.sharding import PartitionSpec as P


def per_device(sources, targets, enc_weight, enc_bias, dec_weight, pair_mask):
    layer_count = dec_weight.shape[1]
    tok_total = sources.shape[1]
    width = sources.shape[2]
    rows_local = targets.shape[1]
    pre = jnp.dot(sources[0], enc_weight[0], preferred_element_type=jnp.float32) + enc_bias[0]
    latent = jnp.maximum(pre, 0.0).astype(jnp.bfloat16)
    latent_all = lax.all_gather(latent[None], "tgt", axis=0, tiled=True)
    owner = lax.axis_index("tgt")
    mask_row = lax.dynamic_index_in_dim(pair_mask, owner, 0, keepdims=False)
    total = jnp.zeros((tok_total, width), jnp.float32)
    for recon_source in range(layer_count):
        rows = latent_all[recon_source]
        recon_weight = mask_row[recon_source].astype(jnp.float32)
        total = total + recon_weight * jnp.dot(
            rows, dec_weight[0, recon_source], preferred_element_type=jnp.float32
        )
    whole = lax.psum(total, "feat")
    target_full = lax.all_gather(targets[0], "feat", axis=0, tiled=True)
    err_full = (whole - target_full.astype(jnp.float32)).astype(jnp.bfloat16)
    err_local = lax.dynamic_slice_in_dim(
        err_full, lax.axis_index("feat") * rows_local, rows_local, 0
    )
    terms = []
    for source in range(layer_count):
        weight = mask_row[source].astype(jnp.float32)
        term = weight * lax.dot_general(
            err_full,
            dec_weight[0, source],
            (((1,), (1,)), ((), ())),
            preferred_element_type=jnp.float32,
        )
        terms.append(term)
    stacked = jnp.stack(terms)
    grads = lax.psum_scatter(stacked, "tgt", scatter_dimension=0, tiled=True)
    return (err_local[None], grads.astype(jnp.bfloat16))


def solution(mesh):
    in_specs = (
        P("tgt", None, None),
        P("tgt", "feat", None),
        P("tgt", None, "feat"),
        P("tgt", "feat"),
        P("tgt", None, "feat", None),
        P(),
    )
    out_specs = (P("tgt", "feat", None), P("tgt", None, "feat"))
    return jax.shard_map(
        per_device, mesh=mesh, in_specs=in_specs, out_specs=out_specs, check_vma=False
    )
```

profile of v0, /device:TPU:0, one launch (start us, length us, event | category | flops | bytes accessed | tf_op | source)
XLA Modules:
  0.0 229.5 jit_solution(2481849422864590683)
XLA Ops:
  7.2 0.0 copy-start
  7.2 0.0 all-gather.4.cloned.1.call-start
  7.2 1.0 copy-done
  8.2 5.9 %fusion.77 = bf16[128,2048]{1,0:T(8,128)(2,1)} fusion(bf16[1,2304,2048]{2,1,0:T(8,128)(2,1)} %param.8, bf16[1,128,2304]{2,1,0:T(8,128)(2,1)S(1)} %copy-done, f32[2048]{0:T(1024)} %bitcast.84), kind=kOutput, calls=%fused_computation.44 | convolution fusion | flops 1208745984 | bytes 10559488 | tf_op jit(solution)/shard_map/dot_general | solution.py:12
  14.1 0.0 all-gather.4.cloned.1.call-update
  14.1 0.0 all-reduce.2.cloned.1.call-start
  14.2 0.7 constant_dynamic-slice_fusion
  14.9 0.7 fusion.86
  18.1 21.5 %all-gather.4.cloned.1.call-done = bf16[512,2048]{1,0:T(8,128)(2,1)} async-done(((bf16[128,2048]{1,0:T(8,128)(2,1)}), bf16[512,2048]{1,0:T(8,128)(2,1)}) %all-gather.4.cloned.1.call-update) | async-done | bytes 2097168 | tf_op jit(solution)/shard_map/all_gather | solution.py:14
  39.6 0.0 copy-start.3
  39.6 5.4 %fusion.32 = f32[128,2304]{1,0:T(8,128)S(1)} fusion(bf16[1,4,2048,2304]{3,2,1,0:T(8,128)(2,1)} %param.10, f32[]{:T(128)} %bitcast.5, bf16[512,2048]{1,0:T(8,128)(2,1)} %all-gather.4.cloned.1.call-done), kind=kOutput, calls=%fused_computation.29 | convolution fusion | flops 1208254464 | bytes 11141632 | tf_op jit(solution)/shard_map/dot_general | solution.py:21
  45.0 0.0 copy-done.3
  45.0 5.2 %fusion.29 = f32[128,2304]{1,0:T(8,128)S(1)} fusion(f32[128,2304]{1,0:T(8,128)S(1)} %fusion.32, bf16[1,4,2048,2304]{3,2,1,0:T(8,128)(2,1)} %param.10, f32[]{:T(128)} %bitcast, bf16[512,2048]{1,0:T(8,128)(2,1)S(1)} %copy-done.3), kind=kOutput, calls=%fused_computation.28 | convolution fusion | flops 1208549376 | bytes 12321280 | tf_op jit(solution)/shard_map/dot_general | solution.py:21
  50.2 5.2 %fusion.38 = f32[128,2304]{1,0:T(8,128)S(1)} fusion(f32[128,2304]{1,0:T(8,128)S(1)} %fusion.29, bf16[1,4,2048,2304]{3,2,1,0:T(8,128)(2,1)} %param.10, f32[]{:T(128)} %bitcast.7, bf16[512,2048]{1,0:T(8,128)(2,1)S(1)} %copy-done.3), kind=kOutput, calls=%fused_computation.31 | convolution fusion | flops 1208549376 | bytes 12321280 | tf_op jit(solution)/shard_map/dot_general | solution.py:21
  55.3 0.0 copy-start.2
  55.4 6.3 %fusion.44 = f32[128,2304]{1,0:T(8,128)} fusion(f32[128,2304]{1,0:T(8,128)S(1)} %fusion.38, bf16[1,4,2048,2304]{3,2,1,0:T(8,128)(2,1)} %param.10, f32[]{:T(128)} %bitcast.9, bf16[512,2048]{1,0:T(8,128)(2,1)S(1)} %copy-done.3), kind=kOutput, calls=%fused_computation.33 | convolution fusion | flops 1208549376 | bytes 12321280 | tf_op jit(solution)/shard_map/dot_general | solution.py:21
  61.6 0.0 all-reduce.2.cloned.1.call-update
  61.6 0.0 reduce-scatter.2.cloned.1.call-start
  61.7 0.0 copy-done.2
  61.7 32.9 %all-gather.1 = bf16[1,128,2304]{2,1,0:T(8,128)(2,1)S(1)} all-gather(bf16[1,16,2304]{2,1,0:T(8,128)(2,1)S(1)} %copy-done.2), channel_id=3, replica_groups=mesh['feat'=8,'tgt'=4] {'feat'}, dimensions={1}, use_global_device_ids=true | all-gather | bytes 663552 | tf_op jit(solution)/shard_map/all_gather | solution.py:25
  94.6 51.1 %all-reduce.2.cloned.1.call-done = f32[128,2304]{1,0:T(8,128)} async-done(((f32[128,2304]{1,0:T(8,128)}), f32[128,2304]{1,0:T(8,128)}) %all-reduce.2.cloned.1.call-update) | async-done | bytes 1179664 | tf_op jit(solution)/shard_map/psum | solution.py:24
  145.7 1.4 fusion.80
  147.1 6.8 %fusion.68 = f32[1,128,2048]{2,1,0:T(8,128)S(1)} fusion(bf16[128,2304]{1,0:T(8,128)(2,1)S(1)} %fusion.80, bf16[1,4,2048,2304]{3,2,1,0:T(8,128)(2,1)} %param.10, f32[]{:T(128)} %bitcast.9), kind=kOutput, calls=%fused_computation.41 | convolution fusion | flops 1208221696 | bytes 11076096 | tf_op jit(solution)/shard_map/dot_general | solution.py:33
  153.9 6.8 %fusion.62 = f32[1,128,2048]{2,1,0:T(8,128)S(1)} fusion(bf16[128,2304]{1,0:T(8,128)(2,1)S(1)} %fusion.80, bf16[1,4,2048,2304]{3,2,1,0:T(8,128)(2,1)} %param.10, f32[]{:T(128)} %bitcast.7), kind=kOutput, calls=%fused_computation.39 | convolution fusion | flops 1208221696 | bytes 11076096 | tf_op jit(solution)/shard_map/dot_general | solution.py:33
  160.7 6.8 %fusion.56 = f32[1,128,2048]{2,1,0:T(8,128)S(1)} fusion(bf16[128,2304]{1,0:T(8,128)(2,1)S(1)} %fusion.80, bf16[1,4,2048,2304]{3,2,1,0:T(8,128)(2,1)} %param.10, f32[]{:T(128)} %bitcast.5), kind=kOutput, calls=%fused_computation.37 | convolution fusion | flops 1208221696 | bytes 11076096 | tf_op jit(solution)/shard_map/dot_general | solution.py:33
  167.6 6.8 %fusion.50 = f32[1,128,2048]{2,1,0:T(8,128)S(1)} fusion(bf16[128,2304]{1,0:T(8,128)(2,1)S(1)} %fusion.80, bf16[1,4,2048,2304]{3,2,1,0:T(8,128)(2,1)} %param.10, f32[]{:T(128)} %bitcast), kind=kOutput, calls=%fused_computation.35 | convolution fusion | flops 1208221696 | bytes 11076096 | tf_op jit(solution)/shard_map/dot_general | solution.py:33
  174.4 0.0 copy-start.1
  174.4 2.4 %pad_maximum_fusion = f32[4,128,2048]{2,1,0:T(8,128)} fusion(f32[1,128,2048]{2,1,0:T(8,128)S(1)} %fusion.68, f32[1,128,2048]{2,1,0:T(8,128)S(1)} %fusion.62, f32[1,128,2048]{2,1,0:T(8,128)S(1)} %fusion.56, f32[1,128,2048]{2,1,0:T(8,128)S(1)} %fusion.50), kind=kLoop, calls=%fused_computation.26 | loop fusion | flops 3145728 | bytes 8388608 | tf_op jit(solution)/shard_map/stack | solution.py:40
  176.8 0.0 reduce-scatter.2.cloned.1.call-update
  176.8 0.6 dynamic-slice_bitcast_fusion
  177.5 43.4 %reduce-scatter.2.cloned.1.call-done = f32[1,128,2048]{2,1,0:T(8,128)} async-done(((f32[4,128,2048]{2,1,0:T(8,128)}), f32[1,128,2048]{2,1,0:T(8,128)}) %reduce-scatter.2.cloned.1.call-update) | async-done | bytes 1048592 | tf_op jit(solution)/shard_map/reduce_scatter | solution.py:41
  220.8 2.1 convert_element_type.51
  222.9 0.0 copy-done.1
Async XLA Ops:
  7.2 1.1 copy-start
  7.2 32.4 %all-gather.4.cloned.1.call-start = ((), (), s32[]{:S(2)}) async-start(), calls=%async_computation.3 | async-start | bytes 2621440 | tf_op jit(solution)/shard_map/all_gather | solution.py:14
  14.1 131.6 %all-reduce.2.cloned.1.call-start = ((), (), s32[]{:S(2)}) async-start(), calls=%async_computation.1 | async-start | bytes 2359296 | tf_op jit(solution)/shard_map/psum | solution.py:24
  39.6 5.4 %copy-start.3 = (bf16[512,2048]{1,0:T(8,128)(2,1)S(1)}, bf16[512,2048]{1,0:T(8,128)(2,1)}, u32[]{:S(2)}) copy-start(bf16[512,2048]{1,0:T(8,128)(2,1)} %all-gather.4.cloned.1.call-done) | copy-start | bytes 6291460
  55.3 6.4 %copy-start.2 = (bf16[1,16,2304]{2,1,0:T(8,128)(2,1)S(1)}, bf16[1,16,2304]{2,1,0:T(8,128)(2,1)}, u32[]{:S(2)}) copy-start(bf16[1,16,2304]{2,1,0:T(8,128)(2,1)} %param.7) | copy-start | bytes 221188
  61.6 159.2 %reduce-scatter.2.cloned.1.call-start = ((), (), s32[]{:S(2)}) async-start(), calls=%async_computation.2 | async-start | bytes 5242880 | tf_op jit(solution)/shard_map/reduce_scatter | solution.py:41
  174.4 48.6 %copy-start.1 = (bf16[1,128,2304]{2,1,0:T(8,128)(2,1)S(1)}, bf16[1,128,2304]{2,1,0:T(8,128)(2,1)}, u32[]{:S(2)}) copy-start(bf16[1,128,2304]{2,1,0:T(8,128)(2,1)} %param.6) | copy-start | bytes 1769476
Sparse Core Ops, SparseCore 0:
  14.3 25.2 all-gather.3
  61.8 83.9 all-reduce.1
  177.0 43.8 reduce-scatter.1
where the time goes:
time: 230 us; the launch traced here: 229 us
  waiting for transfers between devices  116 us (50%)
  matrix products  55.1 us (24%)
  blocking collectives  32.9 us (14%)
  between operations  16.4 us (7%)
  other arithmetic  5.89 us (3%)
  local copies, waits for them, and re-layouts  3.02 us (1%)
    psum x1, waiting for transfers between devices, per_device(): whole = lax.psum(total, 'feat')  51.1 us
    reduce_scatter x1, waiting for transfers between devices, per_device(): grads = lax.psum_scatter(stacked, 'tgt', scatter_dimension=0, tiled=True)  43.4 us
    all_gather x1, blocking collectives, per_device(): target_full = lax.all_gather(targets[0], 'feat', axis=0, tiled=True)  32.9 us
    dot_general x4, matrix products, per_device(): lax.dot_general(err_full, dec_weight[0, source], (((1,), (1,)), ((), ()))...  27.2 us
    dot_general x4, matrix products, per_device(): jnp.dot(rows, dec_weight[0, recon_source], preferred_element_type=jnp.flo...  22 us
    all_gather x1, waiting for transfers between devices, per_device(): latent_all = lax.all_gather(latent[None], 'tgt', axis=0, tiled=True)  21.5 us
    dot_general x1, matrix products, per_device(): jnp.dot(sources[0], enc_weight[0], preferred_element_type=jnp.float32)  5.88 us
  transfers between devices with their start and end apart: 3, of which 3 were waited for; matrix products, arithmetic and copies ran while one was open for 1% of the time, Pallas kernels for 0%

commit v1 on v0

--- a/solution.py
+++ b/solution.py
@@ -1,7 +1,394 @@
+import functools
+import math
+
 import jax
 import jax.numpy as jnp
 from jax import lax
+from jax.experimental import pallas as pl
+from jax.experimental.pallas import tpu as pltpu
 from jax.sharding import PartitionSpec as P
+
+MESH = pl.DeviceIdType.MESH
+F32 = jnp.float32
+BF16 = jnp.bfloat16
+PIECES = 4
+CHUNKS = 2
+
+
+def kernel(nf, nt, mask_ref, src_ref, tgt_ref, enc_hbm, bias_ref, dec_hbm, err_ref, grad_ref,
+           enc, dec, lat, acc, xsend, xrecv, zsend, zrecv, errbuf, errmat, errkeep,
+           ssend, srecv, ysend, yrecv, yown, dsend, drecv, gfin,
+           enc_sem, dec_sem, a_recv, a_sib, a_y, a_fwd,
+           rx_s, rx_r, rz_s, rz_r, gz_s, gx_s, g_r,
+           cs_s, cs_r, cy_s, cy_r, cd_s, cd_r):
+    np_, nc, nz = lat.shape[1], xsend.shape[0], nf // 2
+    fp = lat.shape[3]
+    width = src_ref.shape[2]
+    block = tgt_ref.shape[1]
+    rows = block // nc
+    part = width // nc
+    f = lax.axis_index("feat")
+    t = lax.axis_index("tgt")
+    x, z = lax.rem(f, 2), f // 2
+    core, y = lax.rem(t, 2), t // 2
+    sib = (f, t + 1 - 2 * core)
+    ypeer = (f, lax.rem(t + 2, nt))
+    xpeer = (f + 1 - 2 * x, t)
+
+    def zdev(d):
+        return lax.rem(z + d, nz)
+
+    def enc_copy(p):
+        cols = pl.ds(pl.multiple_of(p * fp, fp), fp)
+        return pltpu.make_async_copy(enc_hbm.at[0, :, cols], enc.at[p], enc_sem.at[p])
+
+    def dec_copy(s, p):
+        rws = pl.ds(pl.multiple_of(p * fp, fp), fp)
+        return pltpu.make_async_copy(dec_hbm.at[0, s, rws, :], dec.at[s, p], dec_sem.at[s, p])
+
+    def remote(src, dst, ss, rs, dev):
+        return pltpu.make_async_remote_copy(
+            src_ref=src, dst_ref=dst, send_sem=ss, recv_sem=rs, device_id=dev, device_id_type=MESH)
+
+    def each(body, n=np_):
+        def step(i, carry):
+            body(i)
+            return carry
+        lax.fori_loop(0, n, step, 0)
+
+    each(lambda p: enc_copy(p).start())
+    each(lambda p: dec_copy(t, p).start())
+
+    @pl.when(core == 1)
+    def _():
+        each(lambda p: dec_copy(t - 1, p).start())
+
+    @pl.when(y == 1)
+    def _():
+        def go(p):
+            dec_copy(core, p).start()
+            dec_copy(1 - core, p).start()
+        each(go)
+
+    barrier = pltpu.get_barrier_semaphore()
+    peers = [sib, ypeer, xpeer] + [(zdev(d) * 2 + x, t) for d in range(1, nz)]
+    for dev in peers:
+        pl.semaphore_signal(barrier, inc=1, device_id=dev, device_id_type=MESH)
+    pl.semaphore_wait(barrier, len(peers))
+
+    def lat_to_sib(p):
+        return remote(lat.at[t, p], lat.at[t, p], a_sib.at[p], a_recv.at[t, p], sib)
+
+    def lat_to_y(p):
+        return remote(lat.at[t, p], lat.at[t, p], a_y.at[p], a_recv.at[t, p], ypeer)
+
+    def lat_forward(p):
+        return remote(lat.at[core, p], lat.at[core, p], a_fwd.at[p], a_recv.at[core, p], sib)
+
+    def lat_wait(s, p):
+        remote(lat.at[s, p], lat.at[s, p], a_fwd.at[p], a_recv.at[s, p], sib).wait_recv()
+
+    def encode(p):
+        enc_copy(p).wait()
+        pre = jnp.dot(src_ref[0], enc[p], preferred_element_type=F32)
+        cols = pl.ds(pl.multiple_of(p * fp, fp), fp)
+        lat[t, p] = jnp.maximum(pre + bias_ref[:, cols], 0.0).astype(BF16)
+
+        @pl.when(y == 0)
+        def _():
+            lat_to_y(p).start()
+
+        @pl.when(core == 0)
+        def _():
+            lat_to_sib(p).start()
+    each(encode)
+
+    def decode(s, p, first=False):
+        dec_copy(s, p).wait()
+        scale = mask_ref[t, s].astype(F32).astype(BF16)
+        left = lat[s, p] * scale
+        step = 256 if width % 256 == 0 else 128
+        for n in range(0, width, step):
+            got = jnp.dot(left, dec[s, p, :, n:n + step], preferred_element_type=F32)
+            if first:
+                acc[:, n:n + step] = got
+            else:
+                acc[:, n:n + step] += got
+
+    decode(t, 0, True)
+    each(lambda i: decode(t, i + 1), np_ - 1)
+
+    @pl.when(core == 1)
+    def _():
+        def go(p):
+            lat_wait(t - 1, p)
+            decode(t - 1, p)
+        each(go)
+
+    @pl.when(y == 1)
+    def _():
+        lat_wait(core, 0)
+        lat_forward(0).start()
+        decode(core, 0)
+
+        def go(i):
+            lat_wait(core, i + 1)
+            lat_forward(i + 1).start()
+            decode(core, i + 1)
+            lat_wait(1 - core, i)
+            decode(1 - core, i)
+        each(go, np_ - 1)
+        lat_wait(1 - core, np_ - 1)
+        decode(1 - core, np_ - 1)
+
+    def pack(v):
+        if nc == 1:
+            return v.astype(BF16)
+        return jnp.concatenate([v[:, j * part:(j + 1) * part] for j in range(nc)], axis=0).astype(BF16)
+
+    def unpack(v):
+        v = v.astype(F32)
+        if nc == 1:
+            return v
+        return jnp.concatenate([v[j * rows:(j + 1) * rows] for j in range(nc)], axis=1)
+
+    def mine(c, g):
+        return acc[pl.ds(pl.multiple_of(g * block + c * rows, rows), rows), :]
+
+    def rx(c, k):
+        return remote(xsend.at[c, k], xrecv.at[c, k], rx_s.at[c, k], rx_r.at[c, k], xpeer)
+
+    def rz(c, d):
+        to = zdev(d)
+        return remote(zsend.at[c, to], zrecv.at[c, z], rz_s.at[c, to], rz_r.at[c, z], (to * 2 + x, t))
+
+    def rz_wait(c, d):
+        fr = zdev(d)
+        remote(zsend.at[c, fr], zrecv.at[c, fr], rz_s.at[c, fr], rz_r.at[c, fr], xpeer).wait_recv()
+
+    def sum_x(c):
+        for d in list(range(1, nz)) + [0]:
+            k = zdev(d)
+            xsend[c, k] = pack(mine(c, k * 2 + 1 - x))
+            rx(c, k).start()
+
+    def sum_z(c):
+        for d in range(1, nz):
+            k = zdev(d)
+            rx(c, k).wait_recv()
+            zsend[c, k] = pack(mine(c, k * 2 + x) + unpack(xrecv[c, k]))
+            rz(c, d).start()
+
+    def gather_z(c, d):
+        return remote(errbuf.at[c, f], errbuf.at[c, f], gz_s.at[c, d - 1], g_r.at[c, f], (zdev(d) * 2 + x, t))
+
+    def gather_x(c, k):
+        g = k * 2 + x
+        return remote(errbuf.at[c, g], errbuf.at[c, g], gx_s.at[c, k], g_r.at[c, g], xpeer)
+
+    def gather_wait(c, g):
+        remote(errbuf.at[c, g], errbuf.at[c, g], gx_s.at[c, 0], g_r.at[c, g], xpeer).wait_recv()
+
+    def finish(c):
+        rx(c, z).wait_recv()
+        total = mine(c, z * 2 + x) + unpack(xrecv[c, z])
+        for d in range(1, nz):
+            rz_wait(c, d)
+            total = total + unpack(zrecv[c, zdev(d)])
+        err = total - tgt_ref[0].astype(F32)[c * rows:(c + 1) * rows]
+        errkeep[pl.ds(c * rows, rows), :] = err
+        errbuf[c, f] = pack(err)
+        for d in range(1, nz):
+            gather_z(c, d).start()
+        gather_x(c, z).start()
+
+    def forward(c):
+        for d in range(1, nz):
+            k = zdev(d)
+            gather_wait(c, k * 2 + x)
+            gather_x(c, k).start()
+
+    def collect(c):
+        for d in range(nz):
+            gather_wait(c, zdev(d) * 2 + 1 - x)
+        group = math.lcm(rows, 16) // rows
+        for g in range(0, nf, group):
+            value = jnp.concatenate([unpack(errbuf[c, g + j]) for j in range(group)], axis=0)
+            errmat[c, g * rows:(g + group) * rows, :] = value.astype(BF16)
+
+    def term(c, s, p):
+        scale = mask_ref[t, s].astype(F32)
+        return scale * lax.dot_general(
+            errmat[c], dec[s, p], (((1,), (1,)), ((), ())), preferred_element_type=F32)
+
+    def to_sib(c, p):
+        return remote(ssend.at[c, p], srecv.at[c, p], cs_s.at[c, p], cs_r.at[c, p], sib)
+
+    def to_y(c, p):
+        return remote(ysend.at[c, p], yrecv.at[c, p], cy_s.at[c, p], cy_r.at[c, p], ypeer)
+
+    def down(c, p):
+        return remote(dsend.at[c, p], drecv.at[c, p], cd_s.at[c, p], cd_r.at[c, p], sib)
+
+    def grads_y(c):
+        @pl.when(y == 1)
+        def _():
+            def give(p):
+                ssend[c, p] = term(c, 1 - core, p).astype(BF16)
+                to_sib(c, p).start()
+                yown[p] = term(c, core, p)
+
+            def pass_on(p):
+                to_sib(c, p).wait_recv()
+                ysend[c, p] = (yown[p] + srecv[c, p].astype(F32)).astype(BF16)
+                to_y(c, p).start()
+
+            give(0)
+
+            def go(i):
+                give(i + 1)
+                pass_on(i)
+            each(go, np_ - 1)
+            pass_on(np_ - 1)
+
+    def grads_pair(c):
+        @pl.when(core == 1)
+        def _():
+            def go(p):
+                dsend[c, p] = term(c, t - 1, p).astype(BF16)
+                down(c, p).start()
+            each(go)
+
+        def own(p):
+            gfin[c, p] = term(c, t, p)
+        each(own)
+
+    def land(p):
+        @pl.when(core == 0)
+        def _():
+            for c in range(nc):
+                down(c, p).wait_recv()
+                gfin[c, p] += drecv[c, p].astype(F32)
+
+        @pl.when(y == 0)
+        def _():
+            for c in range(nc):
+                to_y(c, p).wait_recv()
+                gfin[c, p] += yrecv[c, p].astype(F32)
+        cols = pl.ds(pl.multiple_of(p * fp, fp), fp)
+        for g in range(nf):
+            value = jnp.concatenate([gfin[c, p, g * rows:(g + 1) * rows, :] for c in range(nc)], axis=0)
+            grad_ref[0, g * block:(g + 1) * block, cols] = value.astype(BF16)
+
+    sum_x(0)
+    sum_z(0)
+    for c in range(1, nc):
+        sum_x(c)
+    for c in range(nc):
+        finish(c)
+        if c + 1 < nc:
+            sum_z(c + 1)
+        if c == 0:
+            forward(0)
+    collect(0)
+    grads_y(0)
+    for c in range(1, nc):
+        forward(c)
+        collect(c)
+        grads_y(c)
+    for c in range(nc):
+        grads_pair(c)
+    err_ref[0] = errkeep[...].astype(BF16)
+    each(land)
+
+    def drain(p):
+        @pl.when(y == 0)
+        def _():
+            lat_to_y(p).wait_send()
+
+        @pl.when(core == 0)
+        def _():
+            lat_to_sib(p).wait_send()
+
+        @pl.when(y == 1)
+        def _():
+            lat_forward(p).wait_send()
+            for c in range(nc):
+                to_sib(c, p).wait_send()
+                to_y(c, p).wait_send()
+
+        @pl.when(core == 1)
+        def _():
+            for c in range(nc):
+                down(c, p).wait_send()
+    each(drain)
+    for c in range(nc):
+        for d in range(nz):
+            rx(c, zdev(d)).wait_send()
+            gather_x(c, zdev(d)).wait_send()
+            if d:
+                rz(c, d).wait_send()
+                gather_z(c, d).wait_send()
+
+
+def fused(nf, nt, sources, targets, enc_weight, enc_bias, dec_weight, pair_mask):
+    tok, width = sources.shape[1:]
+    local = enc_weight.shape[2]
+    layers = dec_weight.shape[1]
+    block = targets.shape[1]
+    np_, nc, nz = PIECES, CHUNKS, nf // 2
+    fp = local // np_
+    half = tok // nc
+    part = width // nc
+    vm = pltpu.VMEM
+    dma = pltpu.SemaphoreType.DMA
+    anywhere = pl.BlockSpec(memory_space=pl.ANY)
+    inside = pl.BlockSpec(memory_space=pltpu.VMEM)
+    piece = (nc, np_, half, fp)
+    return pl.pallas_call(
+        functools.partial(kernel, nf, nt),
+        out_shape=(
+            jax.ShapeDtypeStruct(targets.shape, BF16),
+            jax.ShapeDtypeStruct((1, tok, local), BF16),
+        ),
+        in_specs=[pl.BlockSpec(memory_space=pltpu.SMEM), inside, inside, anywhere, inside, anywhere],
+        out_specs=(inside, inside),
+        scratch_shapes=[
+            vm((np_, width, fp), BF16),
+            vm((layers, np_, fp, width), BF16),
+            vm((layers, np_, tok, fp), BF16),
+            vm((tok, width), F32),
+            vm((nc, nz, block, part), BF16),
+            vm((nc, nz, block, part), BF16),
+            vm((nc, nz, block, part), BF16),
+            vm((nc, nz, block, part), BF16),
+            vm((nc, nf, block, part), BF16),
+            vm((nc, half, width), BF16),
+            vm((block, width), F32),
+            vm(piece, BF16), vm(piece, BF16), vm(piece, BF16), vm(piece, BF16),
+            vm((np_, half, fp), F32),
+            vm(piece, BF16), vm(piece, BF16),
+            vm(piece, F32),
+            dma((np_,)), dma((layers, np_)), dma((layers, np_)), dma((np_,)), dma((np_,)), dma((np_,)),
+            dma((nc, nz)), dma((nc, nz)), dma((nc, nz)), dma((nc, nz)),
+            dma((nc, nz)), dma((nc, nz)), dma((nc, nf)),
+            dma((nc, np_)), dma((nc, np_)), dma((nc, np_)), dma((nc, np_)), dma((nc, np_)), dma((nc, np_)),
+        ],
+        compiler_params=pltpu.CompilerParams(
+            collective_id=0, has_side_effects=True, vmem_limit_bytes=63 * 1024 * 1024),
+        cost_estimate=pl.CostEstimate(
+            flops=2 * tok * width * local * (1 + 2 * layers),
+            bytes_accessed=2 * width * local * (1 + layers), transcendentals=0),
+    )(pair_mask, sources, targets, enc_weight, enc_bias, dec_weight)
+
+
+def fits(nf, nt, tok, width, local, layers):
+    block = tok // nf
+    return (
+        nt == 4 and layers == 4 and nf % 2 == 0 and tok % nf == 0 and block % 16 == 0
+        and local % (PIECES * 128) == 0 and width % (CHUNKS * 128) == 0
+        and 2 * width * local * (1 + layers) + 14 * tok * local * 2 <= 56 * 1024 * 1024
+    )
 
 
 def per_device(sources, targets, enc_weight, enc_bias, dec_weight, pair_mask):
@@ -52,6 +439,15 @@
         P(),
     )
     out_specs = (P("tgt", "feat", None), P("tgt", None, "feat"))
+    nf, nt = mesh.shape["feat"], mesh.shape["tgt"]
+
+    def local(sources, targets, enc_weight, enc_bias, dec_weight, pair_mask):
+        tok, width = sources.shape[1:]
+        args = (sources, targets, enc_weight, enc_bias, dec_weight, pair_mask)
+        if fits(nf, nt, tok, width, enc_weight.shape[2], dec_weight.shape[1]):
+            return fused(nf, nt, *args)
+        return per_device(*args)
+
     return jax.shard_map(
-        per_device, mesh=mesh, in_specs=in_specs, out_specs=out_specs, check_vma=False
+        local, mesh=mesh, in_specs=in_specs, out_specs=out_specs, check_vma=False
     )

time: 230 us -> 75.3 us (0.33)
  the two profiles are of different devices: /device:TPU:0 before, /device:TPU:29 now
where the time goes in v1:
time: 75.3 us; the launch traced here: 75 us
  Pallas kernels  71 us (94%)
  local copies, waits for them, and re-layouts  3.4 us (5%)
    pallas_call x1, Pallas kernels, fused(): pl.pallas_call(functools.partial(kernel, nf, nt), out_shape=(jax.ShapeDty...  71 us
    unnamed x2, local copies, waits for them, and re-layouts  3.4 us

profile of v1, /device:TPU:29, one launch (start us, length us, event | category | flops | bytes accessed | tf_op | source)
XLA Modules:
  0.0 75.0 jit_solution(9108221990772432855)
XLA Ops:
  0.6 71.0 %shard_map.77 = (bf16[1,16,2304]{2,1,0:T(8,128)(2,1)}, bf16[1,128,2048]{2,1,0:T(8,128)(2,1)}) custom-call(s32[4,4]{1,0:T(4,128)} %mask_ref.1, bf16[1,128,2304]{2,1,0:T(8,128)(2,1)} %src_ref.1, bf16[1,16,2304]{2,1,0:T(8,128)(2,1)} %tgt_ref.1, bf16[1,2304,2048]{2,1,0:T(8,128)(2,1)} %enc_hbm.1, f32[1,2048]{1,0:T(1,128)} %bias_ref.1, ...), custom_call_target="tpu_custom_call" | custom-call | flops 10871635968 | bytes 47185920 | tf_op jit(solution)/shard_map/pallas_call | solution.py:348
  71.6 1.5 %copy.10 = bf16[1,16,2304]{2,1,0:T(8,128)(2,1)} copy(bf16[1,16,2304]{2,1,0:T(8,128)(2,1)} %get-tuple-element.4) | data formatting | bytes 147456
  73.1 1.9 %copy.11 = bf16[1,128,2048]{2,1,0:T(8,128)(2,1)} copy(bf16[1,128,2048]{2,1,0:T(8,128)(2,1)} %get-tuple-element.5) | data formatting | bytes 1048576

commit v2 on v1

--- a/solution.py
+++ b/solution.py
@@ -13,10 +13,12 @@
 BF16 = jnp.bfloat16
 PIECES = 4
 CHUNKS = 2
+WINDOW = 4
+SWAP = False
 
 
 def kernel(nf, nt, mask_ref, src_ref, tgt_ref, enc_hbm, bias_ref, dec_hbm, err_ref, grad_ref,
-           enc, dec, lat, acc, xsend, xrecv, zsend, zrecv, errbuf, errmat, errkeep,
+           enc, dec, lat, acc, xsend, xrecv, zsend, zrecv, errbuf, errmat,
            ssend, srecv, ysend, yrecv, yown, dsend, drecv, gfin,
            enc_sem, dec_sem, a_recv, a_sib, a_y, a_fwd,
            rx_s, rx_r, rz_s, rz_r, gz_s, gx_s, g_r,
@@ -25,7 +27,6 @@
     fp = lat.shape[3]
     width = src_ref.shape[2]
     block = tgt_ref.shape[1]
-    rows = block // nc
     part = width // nc
     f = lax.axis_index("feat")
     t = lax.axis_index("tgt")
@@ -141,19 +142,8 @@
         lat_wait(1 - core, np_ - 1)
         decode(1 - core, np_ - 1)
 
-    def pack(v):
-        if nc == 1:
-            return v.astype(BF16)
-        return jnp.concatenate([v[:, j * part:(j + 1) * part] for j in range(nc)], axis=0).astype(BF16)
-
-    def unpack(v):
-        v = v.astype(F32)
-        if nc == 1:
-            return v
-        return jnp.concatenate([v[j * rows:(j + 1) * rows] for j in range(nc)], axis=1)
-
     def mine(c, g):
-        return acc[pl.ds(pl.multiple_of(g * block + c * rows, rows), rows), :]
+        return acc[pl.ds(pl.multiple_of(g * block, block), block), c * part:(c + 1) * part]
 
     def rx(c, k):
         return remote(xsend.at[c, k], xrecv.at[c, k], rx_s.at[c, k], rx_r.at[c, k], xpeer)
@@ -166,18 +156,29 @@
         fr = zdev(d)
         remote(zsend.at[c, fr], zrecv.at[c, fr], rz_s.at[c, fr], rz_r.at[c, fr], xpeer).wait_recv()
 
-    def sum_x(c):
-        for d in list(range(1, nz)) + [0]:
-            k = zdev(d)
-            xsend[c, k] = pack(mine(c, k * 2 + 1 - x))
-            rx(c, k).start()
-
-    def sum_z(c):
-        for d in range(1, nz):
+    def sum_feat():
+        order = [(c, d) for c in range(nc) for d in list(range(1, nz)) + [0]]
+
+        def take(i):
+            c, d = order[i]
             k = zdev(d)
             rx(c, k).wait_recv()
-            zsend[c, k] = pack(mine(c, k * 2 + x) + unpack(xrecv[c, k]))
-            rz(c, d).start()
+            if d:
+                zsend[c, k] = (mine(c, k * 2 + x) + xrecv[c, k].astype(F32)).astype(BF16)
+                rz(c, d).start()
+
+        for i, (c, d) in enumerate(order):
+            k = zdev(d)
+            xsend[c, k] = mine(c, k * 2 + 1 - x).astype(BF16)
+            if i >= WINDOW:
+                rx(order[i - WINDOW][0], zdev(order[i - WINDOW][1])).wait_send()
+            rx(c, k).start()
+            if i >= WINDOW - 1:
+                take(i - WINDOW + 1)
+        for i in range(len(order) - WINDOW + 1, len(order)):
+            take(i)
+        for c, d in order[-WINDOW:]:
+            rx(c, zdev(d)).wait_send()
 
     def gather_z(c, d):
         return remote(errbuf.at[c, f], errbuf.at[c, f], gz_s.at[c, d - 1], g_r.at[c, f], (zdev(d) * 2 + x, t))
@@ -189,21 +190,23 @@
     def gather_wait(c, g):
         remote(errbuf.at[c, g], errbuf.at[c, g], gx_s.at[c, 0], g_r.at[c, g], xpeer).wait_recv()
 
+    near = sorted(range(1, nz), key=lambda d: min(d, nz - d))
+
     def finish(c):
-        rx(c, z).wait_recv()
-        total = mine(c, z * 2 + x) + unpack(xrecv[c, z])
+        total = mine(c, z * 2 + x) + xrecv[c, z].astype(F32)
         for d in range(1, nz):
             rz_wait(c, d)
-            total = total + unpack(zrecv[c, zdev(d)])
-        err = total - tgt_ref[0].astype(F32)[c * rows:(c + 1) * rows]
-        errkeep[pl.ds(c * rows, rows), :] = err
-        errbuf[c, f] = pack(err)
-        for d in range(1, nz):
+            total = total + zrecv[c, zdev(d)].astype(F32)
+        cols = slice(c * part, (c + 1) * part)
+        err = (total - tgt_ref[0, :, cols].astype(F32)).astype(BF16)
+        err_ref[0, :, cols] = err
+        errbuf[c, f] = err
+        gather_x(c, z).start()
+        for i, d in enumerate(near):
             gather_z(c, d).start()
-        gather_x(c, z).start()
 
     def forward(c):
-        for d in range(1, nz):
+        for d in near:
             k = zdev(d)
             gather_wait(c, k * 2 + x)
             gather_x(c, k).start()
@@ -211,37 +214,42 @@
     def collect(c):
         for d in range(nz):
             gather_wait(c, zdev(d) * 2 + 1 - x)
-        group = math.lcm(rows, 16) // rows
-        for g in range(0, nf, group):
-            value = jnp.concatenate([unpack(errbuf[c, g + j]) for j in range(group)], axis=0)
-            errmat[c, g * rows:(g + group) * rows, :] = value.astype(BF16)
-
-    def term(c, s, p):
+        cols = slice(c * part, (c + 1) * part)
+        if SWAP:
+            value = jnp.concatenate([errbuf[c, g] for g in range(nf)], axis=0)
+            errmat[cols, :] = value.astype(F32).T.astype(BF16)
+        else:
+            for g in range(nf):
+                errmat[g * block:(g + 1) * block, cols] = errbuf[c, g]
+
+    def term(s, p):
         scale = mask_ref[t, s].astype(F32)
+        if SWAP:
+            return scale * jnp.dot(dec[s, p], errmat[...], preferred_element_type=F32)
         return scale * lax.dot_general(
-            errmat[c], dec[s, p], (((1,), (1,)), ((), ())), preferred_element_type=F32)
-
-    def to_sib(c, p):
-        return remote(ssend.at[c, p], srecv.at[c, p], cs_s.at[c, p], cs_r.at[c, p], sib)
-
-    def to_y(c, p):
-        return remote(ysend.at[c, p], yrecv.at[c, p], cy_s.at[c, p], cy_r.at[c, p], ypeer)
-
-    def down(c, p):
-        return remote(dsend.at[c, p], drecv.at[c, p], cd_s.at[c, p], cd_r.at[c, p], sib)
-
-    def grads_y(c):
+            errmat[...], dec[s, p], (((1,), (1,)), ((), ())), preferred_element_type=F32)
+
+    def to_sib(p):
+        return remote(ssend.at[p], srecv.at[p], cs_s.at[p], cs_r.at[p], sib)
+
+    def to_y(p):
+        return remote(ysend.at[p], yrecv.at[p], cy_s.at[p], cy_r.at[p], ypeer)
+
+    def down(p):
+        return remote(dsend.at[p], drecv.at[p], cd_s.at[p], cd_r.at[p], sib)
+
+    def grads_y():
         @pl.when(y == 1)
         def _():
             def give(p):
-                ssend[c, p] = term(c, 1 - core, p).astype(BF16)
-                to_sib(c, p).start()
-                yown[p] = term(c, core, p)
+                ssend[p] = term(1 - core, p).astype(BF16)
+                to_sib(p).start()
+                yown[p] = term(core, p)
 
             def pass_on(p):
-                to_sib(c, p).wait_recv()
-                ysend[c, p] = (yown[p] + srecv[c, p].astype(F32)).astype(BF16)
-                to_y(c, p).start()
+                to_sib(p).wait_recv()
+                ysend[p] = (yown[p] + srecv[p].astype(F32)).astype(BF16)
+                to_y(p).start()
 
             give(0)
 
@@ -251,54 +259,41 @@
             each(go, np_ - 1)
             pass_on(np_ - 1)
 
-    def grads_pair(c):
+    def grads_pair():
         @pl.when(core == 1)
         def _():
             def go(p):
-                dsend[c, p] = term(c, t - 1, p).astype(BF16)
-                down(c, p).start()
+                dsend[p] = term(t - 1, p).astype(BF16)
+                down(p).start()
             each(go)
 
         def own(p):
-            gfin[c, p] = term(c, t, p)
+            gfin[p] = term(t, p)
         each(own)
 
     def land(p):
         @pl.when(core == 0)
         def _():
-            for c in range(nc):
-                down(c, p).wait_recv()
-                gfin[c, p] += drecv[c, p].astype(F32)
+            down(p).wait_recv()
+            gfin[p] += drecv[p].astype(F32)
 
         @pl.when(y == 0)
         def _():
-            for c in range(nc):
-                to_y(c, p).wait_recv()
-                gfin[c, p] += yrecv[c, p].astype(F32)
+            to_y(p).wait_recv()
+            gfin[p] += yrecv[p].astype(F32)
         cols = pl.ds(pl.multiple_of(p * fp, fp), fp)
-        for g in range(nf):
-            value = jnp.concatenate([gfin[c, p, g * rows:(g + 1) * rows, :] for c in range(nc)], axis=0)
-            grad_ref[0, g * block:(g + 1) * block, cols] = value.astype(BF16)
-
-    sum_x(0)
-    sum_z(0)
-    for c in range(1, nc):
-        sum_x(c)
+        value = gfin[p].T if SWAP else gfin[p]
+        grad_ref[0, :, cols] = value.astype(BF16)
+
+    sum_feat()
     for c in range(nc):
         finish(c)
-        if c + 1 < nc:
-            sum_z(c + 1)
-        if c == 0:
-            forward(0)
-    collect(0)
-    grads_y(0)
-    for c in range(1, nc):
+    for c in range(nc):
         forward(c)
+    for c in range(nc):
         collect(c)
-        grads_y(c)
-    for c in range(nc):
-        grads_pair(c)
-    err_ref[0] = errkeep[...].astype(BF16)
+    grads_y()
+    grads_pair()
     each(land)
 
     def drain(p):
@@ -313,22 +308,20 @@
         @pl.when(y == 1)
         def _():
             lat_forward(p).wait_send()
-            for c in range(nc):
-                to_sib(c, p).wait_send()
-                to_y(c, p).wait_send()
+            to_sib(p).wait_send()
+            to_y(p).wait_send()
 
         @pl.when(core == 1)
         def _():
-            for c in range(nc):
-                down(c, p).wait_send()
+            down(p).wait_send()
     each(drain)
     for c in range(nc):
         for d in range(nz):
-            rx(c, zdev(d)).wait_send()
             gather_x(c, zdev(d)).wait_send()
             if d:
                 rz(c, d).wait_send()
-                gather_z(c, d).wait_send()
+        for d in near:
+            gather_z(c, d).wait_send()
 
 
 def fused(nf, nt, sources, targets, enc_weight, enc_bias, dec_weight, pair_mask):
@@ -338,13 +331,12 @@
     block = targets.shape[1]
     np_, nc, nz = PIECES, CHUNKS, nf // 2
     fp = local // np_
-    half = tok // nc
     part = width // nc
     vm = pltpu.VMEM
     dma = pltpu.SemaphoreType.DMA
     anywhere = pl.BlockSpec(memory_space=pl.ANY)
     inside = pl.BlockSpec(memory_space=pltpu.VMEM)
-    piece = (nc, np_, half, fp)
+    piece = (np_, fp, tok) if SWAP else (np_, tok, fp)
     return pl.pallas_call(
         functools.partial(kernel, nf, nt),
         out_shape=(
@@ -363,16 +355,15 @@
             vm((nc, nz, block, part), BF16),
             vm((nc, nz, block, part), BF16),
             vm((nc, nf, block, part), BF16),
-            vm((nc, half, width), BF16),
-            vm((block, width), F32),
+            vm((width, tok) if SWAP else (tok, width), BF16),
             vm(piece, BF16), vm(piece, BF16), vm(piece, BF16), vm(piece, BF16),
-            vm((np_, half, fp), F32),
+            vm(piece, F32),
             vm(piece, BF16), vm(piece, BF16),
             vm(piece, F32),
             dma((np_,)), dma((layers, np_)), dma((layers, np_)), dma((np_,)), dma((np_,)), dma((np_,)),
             dma((nc, nz)), dma((nc, nz)), dma((nc, nz)), dma((nc, nz)),
             dma((nc, nz)), dma((nc, nz)), dma((nc, nf)),
-            dma((nc, np_)), dma((nc, np_)), dma((nc, np_)), dma((nc, np_)), dma((nc, np_)), dma((nc, np_)),
+            dma((np_,)), dma((np_,)), dma((np_,)), dma((np_,)), dma((np_,)), dma((np_,)),
         ],
         compiler_params=pltpu.CompilerParams(
             collective_id=0, has_side_effects=True, vmem_limit_bytes=63 * 1024 * 1024),

time: 75.3 us -> 64.2 us (0.85)
  the two profiles are of different devices: /device:TPU:29 before, /device:TPU:0 now
where the time goes in v2:
time: 64.2 us; the launch traced here: 63.9 us
  Pallas kernels  59.9 us (93%)
  local copies, waits for them, and re-layouts  3.4 us (5%)
    pallas_call x1, Pallas kernels, fused(): pl.pallas_call(functools.partial(kernel, nf, nt), out_shape=(jax.ShapeDty...  59.9 us
    unnamed x2, local copies, waits for them, and re-layouts  3.4 us

profile of v2, /device:TPU:0, one launch (start us, length us, event | category | flops | bytes accessed | tf_op | source)
XLA Modules:
  0.0 63.9 jit_solution(6192304657049472964)
XLA Ops:
  0.6 59.9 %shard_map.77 = (bf16[1,16,2304]{2,1,0:T(8,128)(2,1)}, bf16[1,128,2048]{2,1,0:T(8,128)(2,1)}) custom-call(s32[4,4]{1,0:T(4,128)} %mask_ref.1, bf16[1,128,2304]{2,1,0:T(8,128)(2,1)} %src_ref.1, bf16[1,16,2304]{2,1,0:T(8,128)(2,1)} %tgt_ref.1, bf16[1,2304,2048]{2,1,0:T(8,128)(2,1)} %enc_hbm.1, f32[1,2048]{1,0:T(1,128)} %bias_ref.1, ...), custom_call_target="tpu_custom_call" | custom-call | flops 10871635968 | bytes 47185920 | tf_op jit(solution)/shard_map/pallas_call | solution.py:340
  60.5 1.5 %copy.10 = bf16[1,16,2304]{2,1,0:T(8,128)(2,1)} copy(bf16[1,16,2304]{2,1,0:T(8,128)(2,1)} %get-tuple-element.4) | data formatting | bytes 147456
  62.0 1.9 %copy.11 = bf16[1,128,2048]{2,1,0:T(8,128)(2,1)} copy(bf16[1,128,2048]{2,1,0:T(8,128)(2,1)} %get-tuple-element.5) | data formatting | bytes 1048576
